TPU v7x, 32 devices: a whole 2x2x4 slice. The times are simulated.
32 devices in a mesh: grp: 2 (over y), wide: 8 (over z, x), sec: 2 (over core).
Axes of the slice: x: 2, y: 2, z: 4, core: 2. Of those that a mesh axis runs over, the one named last changes fastest.
Arguments:
- dosage: bfloat16 [4096, 16384], P(('sec', 'wide'), 'grp'), parts along dimension 1, may hold values from 0 to 2
- weights: bfloat16 [20, 24, 128, 128], P(None, 'sec'), may hold values from -0.109375 to 0.109375
- blocks: int32 [20, 24], P(None, 'sec'), may hold values from 0 to 15, as said below
- flips: int32 [4096], P('sec'), may hold values 0 or 1
Outputs:
- scores: float32 [16384, 2560], P(('grp', 'wide'), 'sec'), parts along dimension 0
There are 2 independent parts, one for each index of `grp`. A program takes and returns all parts, laid end to end along the dimension named above; an argument that names none is the same for every part. Nothing has to cross between parts.
Inputs may be any that keep to these rules, and one draw needn't show every extreme that they name: blocks[t, k] counts within the section of variants k // 12; within one tile and one section the 12 block numbers are distinct.
All inputs are finite; a program needn't handle non-finite values. No bound on the sum of `flips` on one device may be relied on, other than what follows from the above.
Results may differ from a plain program's by a relative error of at most 0.0003.
Values may be sent and summed in bfloat16 or wider, within the bound.
A program may use at most 128 MiB of HBM per device.

v0:
```python
import jax
import jax.numpy as jnp
from jax import lax
from jax.sharding import PartitionSpec as P


def body(dosage, weights, blocks, flips):
    section = lax.all_to_all(dosage, "wide", split_axis=1, concat_axis=0, tiled=True)
    block_size = weights.shape[2]
    tile_count = weights.shape[0]
    section_count = flips.shape[0] // block_size
    flip_rows = flips.reshape(-1, block_size)[blocks]
    signed = jnp.where(flip_rows[..., None] == 1, -weights, weights)
    offset = 2.0 * jnp.einsum(
        "tkr,tkrc->tc", flip_rows.astype(jnp.bfloat16), weights, preferred_element_type=jnp.float32
    )
    one_hot = (
        blocks[..., None] == jnp.arange(section_count, dtype=jnp.int32)[None, None, :]
    ).astype(jnp.bfloat16)
    dense = jnp.einsum("tkb,tkrc->brtc", one_hot, signed, preferred_element_type=jnp.float32)
    dense = dense.astype(jnp.bfloat16).reshape(section_count * block_size, tile_count * block_size)
    partial_scores = jnp.einsum("vs,vc->sc", section, dense, preferred_element_type=jnp.float32)
    partial_scores = partial_scores + offset.reshape(1, -1)
    return lax.psum_scatter(partial_scores, "sec", scatter_dimension=1, tiled=True)


def solution(mesh):
    in_specs = (P(("sec", "wide"), "grp"), P(None, "sec", None, None), P(None, "sec"), P("sec"))
    out_specs = P(("grp", "wide"), "sec")
    return jax.shard_map(body, mesh=mesh, in_specs=in_specs, out_specs=out_specs, check_vma=False)
```

profile of v0, /device:TPU:0, one launch (start us, length us, event | category | flops | bytes accessed | tf_op | source)
XLA Modules:
  0.0 167.8 jit_solution(12323514043267406251)
XLA Ops:
  6.5 0.0 copy-start
  6.5 0.0 copy-start.2
  6.5 6.4 %copy.17 = bf16[256,8192]{0,1:T(8,128)(2,1)} copy(bf16[256,8192]{1,0:T(8,128)(2,1)} %param.4) | data formatting | bytes 8388608 | tf_op args[0]
  12.9 7.3 %all-to-all-start = ((bf16[256,8,1024]{0,2,1:T(8,128)(2,1)}), bf16[256,8,1024]{0,2,1:T(8,128)(2,1)}, u32[]{:S(2)}, u32[]{:S(2)}) async-start(bf16[256,8,1024]{0,2,1:T(8,128)(2,1)} %bitcast.32), calls=%async_computation | async-start | bytes 8388608 | tf_op jit(solution)/shard_map/all_to_all | solution.py:8
  20.2 0.0 reduce-scatter.2.cloned.1.call-start
  20.2 0.0 copy-done.2
  20.2 0.1 copy.14
  20.3 0.1 copy.13
  20.4 0.1 reshape.20
  20.5 0.0 copy-done
  20.5 0.7 gather_fusion
  21.4 6.8 %negate_select_fusion = bf16[20,12,128,128]{3,2,1,0:T(8,128)(2,1)S(1)} fusion(bf16[20,12,128,128]{3,2,1,0:T(8,128)(2,1)} %param.5, pred[20,12,128]{2,1,0:T(8,128)(4,1)S(1)} %reshape.29), kind=kLoop, calls=%fused_computation.1 | loop fusion | flops 7864320 | bytes 15759360 | tf_op jit(solution)/shard_map/jit(_where)/select_n | solution.py:13
  28.2 8.6 %convert_bitcast_fusion = bf16[16,128,20,128]{3,0,1,2:T(8,128)(2,1)} fusion(bf16[20,12,128,128]{3,2,1,0:T(8,128)(2,1)S(1)} %negate_select_fusion, s32[20,12]{1,0:T(8,128)S(1)} %copy.14), kind=kOutput, calls=%fused_computation.8 | convolution fusion | flops 131075840 | bytes 18351040 | tf_op jit(solution)/shard_map/tkb,tkrc->brtc/dot_general | solution.py:20
  36.8 15.6 %copy.16 = bf16[16,128,20,128]{1,0,3,2:T(8,128)(2,1)} copy(bf16[16,128,20,128]{3,0,1,2:T(8,128)(2,1)} %convert_bitcast_fusion) | data formatting | bytes 20971520 | tf_op jit(solution)/shard_map/convert_element_type | solution.py:21
  52.3 4.5 %fusion.13 = f32[20,1,128,1]{2,1,3,0:T(1,128)S(1)} fusion(bf16[20,12,128,1]{2,3,1,0:T(2,128)(2,1)S(1)} %reshape.35, bf16[20,12,128,128]{3,2,1,0:T(8,128)(2,1)} %param.5), kind=kOutput, calls=%fused_computation.17 | convolution fusion | flops 7864320 | bytes 7936000 | tf_op jit(solution)/shard_map/tkr,tkrc->tc/dot_general | solution.py:14
  56.8 56.7 %all-to-all-done = bf16[256,8,1024]{0,2,1:T(8,128)(2,1)} async-done(((bf16[256,8,1024]{0,2,1:T(8,128)(2,1)}), bf16[256,8,1024]{0,2,1:T(8,128)(2,1)}, u32[]{:S(2)}, u32[]{:S(2)}) %all-to-all-start) | async-done | bytes 4194336 | tf_op jit(solution)/shard_map/all_to_all | solution.py:8
  113.5 6.4 %copy.18 = bf16[8,256,1024]{2,1,0:T(8,128)(2,1)} copy(bf16[8,256,1024]{1,2,0:T(8,128)(2,1)} %bitcast.5) | data formatting | bytes 8388608 | tf_op jit(solution)/shard_map/all_to_all | solution.py:8
  119.9 16.9 %add_bitcast_fusion = f32[1024,2560]{0,1:T(8,128)} fusion(bf16[2048,1024]{1,0:T(8,128)(2,1)} %bitcast.34, bf16[320,8,16,128]{3,2,1,0:T(8,128)(2,1)} %bitcast.33, f32[2560]{0:T(1024)S(1)} %fusion.12), kind=kOutput, calls=%fused_computation.7 | convolution fusion | flops 10740039680 | bytes 25176064 | tf_op jit(solution)/shard_map/vs,vc->sc/dot_general | solution.py:22
  136.8 0.0 reduce-scatter.2.cloned.1.call-update
  136.8 0.0 copy-start.1
  136.8 18.3 %reduce-scatter.2.cloned.1.call-done = f32[1024,1280]{0,1:T(8,128)} async-done(((f32[1024,2560]{0,1:T(8,128)}), f32[1024,1280]{0,1:T(8,128)}) %reduce-scatter.2.cloned.1.call-update) | async-done | bytes 5242896 | tf_op jit(solution)/shard_map/reduce_scatter | solution.py:24
  155.1 5.9 %copy.19 = f32[1024,1280]{1,0:T(8,128)} copy(f32[1024,1280]{0,1:T(8,128)} %reduce-scatter.2.cloned.1.call-done) | data formatting | bytes 10485760 | tf_op jit(solution)/shard_map/reduce_scatter | solution.py:24
  160.9 0.0 copy-done.1
  (7 shorter events, 0.1 us)
Async XLA Ops:
  6.5 14.0 %copy-start = (s32[2048]{0:T(1024)S(1)}, s32[2048]{0:T(1024)}, u32[]{:S(2)}) copy-start(s32[2048]{0:T(1024)} %param.7) | copy-start | bytes 24580
  6.5 13.7 %copy-start.2 = (s32[20,12]{0,1:T(8,128)S(1)}, s32[20,12]{0,1:T(8,128)}, u32[]{:S(2)}) copy-start(s32[20,12]{0,1:T(8,128)} %param.6) | copy-start | bytes 2884
  12.9 100.5 %all-to-all-start = ((bf16[256,8,1024]{0,2,1:T(8,128)(2,1)}), bf16[256,8,1024]{0,2,1:T(8,128)(2,1)}, u32[]{:S(2)}, u32[]{:S(2)}) async-start(bf16[256,8,1024]{0,2,1:T(8,128)(2,1)} %bitcast.32), calls=%async_computation | async-start | bytes 8388608 | tf_op jit(solution)/shard_map/all_to_all | solution.py:8
  20.2 134.9 %reduce-scatter.2.cloned.1.call-start = ((), (), s32[]{:S(2)}) async-start(), calls=%async_computation.2 | async-start | bytes 15728640 | tf_op jit(solution)/shard_map/reduce_scatter | solution.py:24
  136.8 24.2 %copy-start.1 = (s32[2048]{0:T(1024)S(1)}, s32[2048]{0:T(1024)}, u32[]{:S(2)}) copy-start(s32[2048]{0:T(1024)} %param.7) | copy-start | bytes 24580
Sparse Core Ops, SparseCore 0:
  136.9 18.1 reduce-scatter.1
where the time goes:
time: 169 us; the launch traced here: 168 us
  waiting for transfers between devices  74.9 us (44%)
  local copies, waits for them, and re-layouts  35.3 us (21%)
  matrix products  29.9 us (18%)
  between operations  13.5 us (8%)
  starting transfers between devices  7.29 us (4%)
  other arithmetic  6.84 us (4%)
    all_to_all x1, waiting for transfers between devices, body(): lax.all_to_all(dosage, 'wide', split_axis=1, concat_axis=0, tiled=True)  56.7 us
    reduce_scatter x1, waiting for transfers between devices, body(): lax.psum_scatter(partial_scores, 'sec', scatter_dimension=1, tiled=True)  18.3 us
    dot_general x1, matrix products, body(): jnp.einsum('vs,vc->sc', section, dense, preferred_element_type=jnp.float32)  16.9 us
    convert_element_type x1, local copies, waits for them, and re-layouts, body(): dense.astype(jnp.bfloat16)  15.6 us
    dot_general x1, matrix products, body(): jnp.einsum('tkb,tkrc->brtc', one_hot, signed, preferred_element_type=jnp....  8.59 us
    all_to_all x1, starting transfers between devices, body(): lax.all_to_all(dosage, 'wide', split_axis=1, concat_axis=0, tiled=True)  7.25 us
    select_n x1, other arithmetic, body(): signed = jnp.where(flip_rows[..., None] == 1, -weights, weights)  6.79 us
    unnamed x8, local copies, waits for them, and re-layouts  6.49 us
  transfers between devices with their start and end apart: 2, of which 2 were waited for; matrix products, arithmetic and copies ran while one was open for 22% of the time, Pallas kernels for 0%

commit v1 on v0

v1 whole, which is shorter than its diff:
```python
import functools

import jax
import jax.numpy as jnp
from jax import lax
from jax.experimental import pallas as pl
from jax.experimental.pallas import tpu as pltpu
from jax.sharding import PartitionSpec as P

MESH = pl.DeviceIdType.MESH
MIB = 1024 * 1024


def partner_of(me, k):
    bit, out = 1, me
    while bit <= k:
        if k & bit:
            out = out + bit - 2 * bit * (lax.rem(lax.div(me, bit), 2))
        bit *= 2
    return out


def kernel(n, chunks, width, dos, wts, blocks, flips, out, x, dense, stage, raw_other, raw_own, sign, off, off_in, xt,
           send_sem, recv_sem, own_sem, fwd_send, fwd_recv, w_sem, d_send, d_recv, o_send, o_recv):
    me = lax.axis_index("wide")
    sec = lax.axis_index("sec")
    grp = lax.axis_index("grp")
    other = 1 - sec
    rows = dos.shape[0]
    samples = chunks * width
    tiles, nnz, block, _ = wts.shape
    half = tiles // 2
    count = flips.shape[0]
    power = n & (n - 1) == 0
    order = list(range(n - 1, 0, -1))
    peers = [partner_of(me, k) if power else lax.rem(me + k, n) for k in order]
    mine = pl.ds(pl.multiple_of(me * rows, rows), rows)

    barrier = pltpu.get_barrier_semaphore()
    for peer in peers:
        pl.semaphore_signal(barrier, inc=1, device_id=(grp, peer, sec), device_id_type=MESH)
    pl.semaphore_signal(barrier, inc=1, device_id=(grp, me, other), device_id_type=MESH)

    load = [
        pltpu.make_async_copy(wts.at[pl.ds(h * half, half)], raw, w_sem.at[i])
        for i, (h, raw) in enumerate(((other, raw_other), (sec, raw_own)))
    ]
    for copy in load:
        copy.start()
    own = [
        pltpu.make_async_copy(
            dos.at[:, pl.ds(pl.multiple_of(me * samples + c * width, width), width)], x.at[c, sec, mine], own_sem.at[c]
        )
        for c in range(chunks)
    ]
    pl.semaphore_wait(barrier, n)

    for c in range(chunks):
        for peer in peers:
            pltpu.make_async_remote_copy(
                src_ref=dos.at[:, pl.ds(pl.multiple_of(peer * samples + c * width, width), width)],
                dst_ref=x.at[c, sec, mine],
                send_sem=send_sem.at[c],
                recv_sem=recv_sem.at[c],
                device_id=(grp, peer, sec),
                device_id_type=MESH,
            ).start()
    for copy in own:
        copy.start()

    for b in range(count):
        row = flips[b : b + 1, :].astype(jnp.float32)
        sign[b] = 1.0 - 2.0 * jnp.transpose(jnp.broadcast_to(row, (block, block)))

    def build(h, raw, put):
        def one(j, _):
            t = h * half + j
            total = jnp.zeros((block, block), jnp.float32)
            for b in range(count):
                at = jnp.int32(0)
                there = jnp.int32(0)
                for k in range(nnz):
                    same = blocks[t, k] == b
                    at = jnp.where(same, jnp.int32(k), at)
                    there = jnp.where(same, jnp.int32(1), there)
                value = raw[j, at].astype(jnp.float32) * there.astype(jnp.float32)
                signs = sign[b]
                total = total + (1.0 - signs) * value
                put(b, j, (value * signs).astype(jnp.bfloat16))
            line = jnp.sum(total, axis=0, keepdims=True)
            off[h, j] = jnp.broadcast_to(line, (8, block))
            return 0

        lax.fori_loop(0, half, one, 0)

    def put_stage(b, j, value):
        stage[b * block : (b + 1) * block, pl.ds(pl.multiple_of(j * block, block), block)] = value

    def put_dense(b, j, value):
        dense[sec, b * block : (b + 1) * block, pl.ds(pl.multiple_of(j * block, block), block)] = value

    load[0].wait()
    build(other, raw_other, put_stage)
    send_dense = pltpu.make_async_remote_copy(
        src_ref=stage, dst_ref=dense.at[sec], send_sem=d_send, recv_sem=d_recv,
        device_id=(grp, me, other), device_id_type=MESH,
    )
    send_off = pltpu.make_async_remote_copy(
        src_ref=off.at[other], dst_ref=off_in, send_sem=o_send, recv_sem=o_recv,
        device_id=(grp, me, other), device_id_type=MESH,
    )
    send_dense.start()
    send_off.start()
    load[1].wait()
    build(sec, raw_own, put_dense)
    pltpu.make_async_copy(stage, dense.at[other], d_recv).wait()
    send_off.wait_recv()

    depth = count * block
    step = 2 * block
    columns = half * block
    wide_n = 2 * block if columns % (2 * block) == 0 else block

    def multiply(c, which, first):
        def turn(i, _):
            r = pl.ds(pl.multiple_of(i * step, step), step)
            xt[:, r] = jnp.transpose(x[c, which, r, :])
            return 0

        lax.fori_loop(0, depth // step, turn, 0)

        def column(i, _):
            at = pl.ds(pl.multiple_of(i * wide_n, wide_n), wide_n)
            value = jnp.dot(xt[...], dense[which, :, at], preferred_element_type=jnp.float32)
            here = slice(c * width, (c + 1) * width)
            if first:
                per = wide_n // block
                line = jnp.concatenate(
                    [(off[sec, i * per + q] + off_in[i * per + q])[0:1, :] for q in range(per)], axis=1
                )
                out[here, at] = value + line
            else:
                out[here, at] += value
            return 0

        lax.fori_loop(0, columns // wide_n, column, 0)

    for c in range(chunks):
        own[c].wait()
        from_peers = x.at[c, sec, pl.ds(0, (n - 1) * rows)]
        pltpu.make_async_copy(from_peers, from_peers, recv_sem.at[c]).wait()
        forward = pltpu.make_async_remote_copy(
            src_ref=x.at[c, sec], dst_ref=x.at[c, sec], send_sem=fwd_send.at[c], recv_sem=fwd_recv.at[c],
            device_id=(grp, me, other), device_id_type=MESH,
        )
        forward.start()
        multiply(c, sec, True)
        pltpu.make_async_copy(x.at[c, sec], x.at[c, other], fwd_recv.at[c]).wait()
        multiply(c, other, False)
        forward.wait_send()

    for c in range(chunks):
        to_peers = x.at[c, sec, pl.ds(0, (n - 1) * rows)]
        pltpu.make_async_copy(to_peers, to_peers, send_sem.at[c]).wait()
    send_dense.wait_send()
    send_off.wait_send()


def solution(mesh):
    n = mesh.shape["wide"]
    chunks = 4

    def body(dosage, weights, blocks, flips):
        tiles, nnz, block, _ = weights.shape
        half = tiles // 2
        rows, everyone = dosage.shape
        samples = everyone // n
        width = samples // chunks
        depth = flips.shape[0]
        count = depth // block
        columns = half * block
        any_space = pl.BlockSpec(memory_space=pl.ANY)
        vmem = pl.BlockSpec(memory_space=pltpu.VMEM)
        return pl.pallas_call(
            functools.partial(kernel, n, chunks, width),
            out_shape=pltpu.VMEM((samples, columns), jnp.float32),
            in_specs=[any_space, any_space, pl.BlockSpec(memory_space=pltpu.SMEM), vmem],
            out_specs=vmem,
            scratch_shapes=[
                pltpu.VMEM((chunks, 2, depth, width), jnp.bfloat16),
                pltpu.VMEM((2, depth, columns), jnp.bfloat16),
                pltpu.VMEM((depth, columns), jnp.bfloat16),
                pltpu.VMEM((half, nnz, block, block), jnp.bfloat16),
                pltpu.VMEM((half, nnz, block, block), jnp.bfloat16),
                pltpu.VMEM((count, block, block), jnp.float32),
                pltpu.VMEM((2, half, 8, block), jnp.float32),
                pltpu.VMEM((half, 8, block), jnp.float32),
                pltpu.VMEM((width, depth), jnp.bfloat16),
                pltpu.SemaphoreType.DMA((chunks,)),
                pltpu.SemaphoreType.DMA((chunks,)),
                pltpu.SemaphoreType.DMA((chunks,)),
                pltpu.SemaphoreType.DMA((chunks,)),
                pltpu.SemaphoreType.DMA((chunks,)),
                pltpu.SemaphoreType.DMA((2,)),
                pltpu.SemaphoreType.DMA,
                pltpu.SemaphoreType.DMA,
                pltpu.SemaphoreType.DMA,
                pltpu.SemaphoreType.DMA,
            ],
            compiler_params=pltpu.CompilerParams(
                collective_id=0, has_side_effects=True, vmem_limit_bytes=50 * MIB
            ),
        )(dosage, weights, blocks, flips.reshape(count, block))

    in_specs = (P(("sec", "wide"), "grp"), P(None, "sec", None, None), P(None, "sec"), P("sec"))
    out_specs = P(("grp", "wide"), "sec")
    return jax.shard_map(body, mesh=mesh, in_specs=in_specs, out_specs=out_specs, check_vma=False)
```

time: 169 us -> 109 us (0.64)
  Pallas kernels: 0 us -> 105 us
  waiting for transfers between devices: 74.9 us -> 0 us
  local copies, waits for them, and re-layouts: 35.3 us -> 3.74 us
  matrix products: 29.9 us -> 0 us
  between operations: 13.5 us -> 0.01 us
  starting transfers between devices: 7.29 us -> 0 us
  other arithmetic: 6.84 us -> 0 us
    pallas_call x0 -> x1, Pallas kernels: none -> 105 us  [body(): pl.pallas_call(functools.partial(kernel, n, chunks, width), out_shape=plt...]
    all_to_all x1 -> x0, waiting for transfers between devices: 56.7 us -> none  [body(): lax.all_to_all(dosage, 'wide', split_axis=1, concat_axis=0, tiled=True)]
    dot_general x3 -> x0, matrix products: 29.9 us -> none  [the longest x1 16.9 us: body(): jnp.einsum('vs,vc->sc', section, dense, preferred_element_type=jnp.float32)]
    reduce_scatter x1 -> x0, waiting for transfers between devices: 18.3 us -> none  [body(): lax.psum_scatter(partial_scores, 'sec', scatter_dimension=1, tiled=True)]
    convert_element_type x2 -> x0, local copies, waits for them, and re-layouts: 15.6 us -> none  [the longest x1 15.6 us: body(): dense.astype(jnp.bfloat16)]
    all_to_all x1 -> x0, starting transfers between devices: 7.25 us -> none  [body(): lax.all_to_all(dosage, 'wide', split_axis=1, concat_axis=0, tiled=True)]
    select_n x2 -> x0, other arithmetic: 6.8 us -> none  [the longest x1 6.79 us: body(): signed = jnp.where(flip_rows[..., None] == 1, -weights, weights)]
    all_to_all x1 -> x0, local copies, waits for them, and re-layouts: 6.43 us -> none  [body(): lax.all_to_all(dosage, 'wide', split_axis=1, concat_axis=0, tiled=True)]
  transfers between devices with their start and end apart: 2 -> 0, of which waited for: 2 -> 0; matrix products, arithmetic and copies ran while one was open for 22% -> 0% of each run, Pallas kernels for 0% -> 0%
where the time goes in v1:
time: 109 us
  Pallas kernels  105 us (96%)
  local copies, waits for them, and re-layouts  3.74 us (3%)
    pallas_call x1, Pallas kernels, body(): pl.pallas_call(functools.partial(kernel, n, chunks, width), out_shape=plt...  105 us
    unnamed x2, local copies, waits for them, and re-layouts  3.74 us

profile of v1, /device:TPU:0, one launch (start us, length us, event | category | flops | bytes accessed | tf_op | source)
XLA Modules:
  0.0 108.6 jit_solution(608610816671608378)
XLA Ops:
  0.0 1.4 %copy.5.blocks = s32[20,12]{1,0:T(8,128)} copy(s32[20,12]{0,1:T(8,128)} %param.6) | data formatting | bytes 1920 | tf_op args[2]
  1.4 104.9 %shard_map.46 = f32[1024,1280]{1,0:T(8,128)S(1)} custom-call(bf16[256,8192]{1,0:T(8,128)(2,1)} %dos.1, bf16[20,12,128,128]{3,2,1,0:T(8,128)(2,1)} %wts.1, s32[20,12]{1,0:T(8,128)} %copy.5.blocks, s32[16,128]{1,0:T(8,128)} %bitcast.1), custom_call_target="tpu_custom_call" | custom-call | tf_op jit(solution)/shard_map/pallas_call | solution.py:184
  106.3 2.4 %copy.7 = f32[1024,1280]{1,0:T(8,128)} copy(f32[1024,1280]{1,0:T(8,128)S(1)} %shard_map.46) | data formatting | bytes 10485760

commit v2 on v1

--- a/solution.py
+++ b/solution.py
@@ -20,19 +20,31 @@
     return out
 
 
-def kernel(n, chunks, width, dos, wts, blocks, flips, out, x, dense, stage, raw_other, raw_own, sign, off, off_in, xt,
-           send_sem, recv_sem, own_sem, fwd_send, fwd_recv, w_sem, d_send, d_recv, o_send, o_recv):
+SHARES = (2, 2, 2, 1, 1)
+
+
+def split(samples, block):
+    unit = samples // sum(SHARES)
+    if samples % sum(SHARES) or unit % block:
+        return (samples,)
+    return tuple(share * unit for share in SHARES)
+
+
+def kernel(n, widths, dos, wts, blocks, flips, out, dense, stage, raw_other, raw_own, sign, off, off_in,
+           send_sem, recv_sem, own_sem, fwd_send, fwd_recv, w_sem, d_send, d_recv, o_send, o_recv, *x):
     me = lax.axis_index("wide")
     sec = lax.axis_index("sec")
     grp = lax.axis_index("grp")
     other = 1 - sec
     rows = dos.shape[0]
-    samples = chunks * width
+    samples = sum(widths)
+    chunks = len(widths)
+    first_of = [sum(widths[:c]) for c in range(chunks)]
     tiles, nnz, block, _ = wts.shape
     half = tiles // 2
     count = flips.shape[0]
     power = n & (n - 1) == 0
-    order = list(range(n - 1, 0, -1))
+    order = list(range(1, n))
     peers = [partner_of(me, k) if power else lax.rem(me + k, n) for k in order]
     mine = pl.ds(pl.multiple_of(me * rows, rows), rows)
 
@@ -49,7 +61,7 @@
         copy.start()
     own = [
         pltpu.make_async_copy(
-            dos.at[:, pl.ds(pl.multiple_of(me * samples + c * width, width), width)], x.at[c, sec, mine], own_sem.at[c]
+            dos.at[:, pl.ds(pl.multiple_of(me * samples + first_of[c], block), widths[c])], x[c].at[sec, mine], own_sem.at[c]
         )
         for c in range(chunks)
     ]
@@ -58,8 +70,8 @@
     for c in range(chunks):
         for peer in peers:
             pltpu.make_async_remote_copy(
-                src_ref=dos.at[:, pl.ds(pl.multiple_of(peer * samples + c * width, width), width)],
-                dst_ref=x.at[c, sec, mine],
+                src_ref=dos.at[:, pl.ds(pl.multiple_of(peer * samples + first_of[c], block), widths[c])],
+                dst_ref=x[c].at[sec, mine],
                 send_sem=send_sem.at[c],
                 recv_sem=recv_sem.at[c],
                 device_id=(grp, peer, sec),
@@ -80,7 +92,7 @@
                 at = jnp.int32(0)
                 there = jnp.int32(0)
                 for k in range(nnz):
-                    same = blocks[t, k] == b
+                    same = blocks[k, t] == b
                     at = jnp.where(same, jnp.int32(k), at)
                     there = jnp.where(same, jnp.int32(1), there)
                 value = raw[j, at].astype(jnp.float32) * there.astype(jnp.float32)
@@ -117,22 +129,16 @@
     send_off.wait_recv()
 
     depth = count * block
-    step = 2 * block
     columns = half * block
     wide_n = 2 * block if columns % (2 * block) == 0 else block
 
     def multiply(c, which, first):
-        def turn(i, _):
-            r = pl.ds(pl.multiple_of(i * step, step), step)
-            xt[:, r] = jnp.transpose(x[c, which, r, :])
-            return 0
-
-        lax.fori_loop(0, depth // step, turn, 0)
+        width = widths[c]
 
         def column(i, _):
             at = pl.ds(pl.multiple_of(i * wide_n, wide_n), wide_n)
-            value = jnp.dot(xt[...], dense[which, :, at], preferred_element_type=jnp.float32)
-            here = slice(c * width, (c + 1) * width)
+            value = lax.dot_general(x[c][which], dense[which, :, at], (((0,), (0,)), ((), ())), preferred_element_type=jnp.float32)
+            here = slice(first_of[c], first_of[c] + width)
             if first:
                 per = wide_n // block
                 line = jnp.concatenate(
@@ -147,20 +153,20 @@
 
     for c in range(chunks):
         own[c].wait()
-        from_peers = x.at[c, sec, pl.ds(0, (n - 1) * rows)]
+        from_peers = x[c].at[sec, pl.ds(0, (n - 1) * rows)]
         pltpu.make_async_copy(from_peers, from_peers, recv_sem.at[c]).wait()
         forward = pltpu.make_async_remote_copy(
-            src_ref=x.at[c, sec], dst_ref=x.at[c, sec], send_sem=fwd_send.at[c], recv_sem=fwd_recv.at[c],
+            src_ref=x[c].at[sec], dst_ref=x[c].at[sec], send_sem=fwd_send.at[c], recv_sem=fwd_recv.at[c],
             device_id=(grp, me, other), device_id_type=MESH,
         )
         forward.start()
         multiply(c, sec, True)
-        pltpu.make_async_copy(x.at[c, sec], x.at[c, other], fwd_recv.at[c]).wait()
+        pltpu.make_async_copy(x[c].at[sec], x[c].at[other], fwd_recv.at[c]).wait()
         multiply(c, other, False)
         forward.wait_send()
 
     for c in range(chunks):
-        to_peers = x.at[c, sec, pl.ds(0, (n - 1) * rows)]
+        to_peers = x[c].at[sec, pl.ds(0, (n - 1) * rows)]
         pltpu.make_async_copy(to_peers, to_peers, send_sem.at[c]).wait()
     send_dense.wait_send()
     send_off.wait_send()
@@ -168,26 +174,25 @@
 
 def solution(mesh):
     n = mesh.shape["wide"]
-    chunks = 4
 
     def body(dosage, weights, blocks, flips):
         tiles, nnz, block, _ = weights.shape
         half = tiles // 2
         rows, everyone = dosage.shape
         samples = everyone // n
-        width = samples // chunks
+        widths = split(samples, block)
+        chunks = len(widths)
         depth = flips.shape[0]
         count = depth // block
         columns = half * block
         any_space = pl.BlockSpec(memory_space=pl.ANY)
         vmem = pl.BlockSpec(memory_space=pltpu.VMEM)
         return pl.pallas_call(
-            functools.partial(kernel, n, chunks, width),
+            functools.partial(kernel, n, widths),
             out_shape=pltpu.VMEM((samples, columns), jnp.float32),
             in_specs=[any_space, any_space, pl.BlockSpec(memory_space=pltpu.SMEM), vmem],
             out_specs=vmem,
             scratch_shapes=[
-                pltpu.VMEM((chunks, 2, depth, width), jnp.bfloat16),
                 pltpu.VMEM((2, depth, columns), jnp.bfloat16),
                 pltpu.VMEM((depth, columns), jnp.bfloat16),
                 pltpu.VMEM((half, nnz, block, block), jnp.bfloat16),
@@ -195,7 +200,6 @@
                 pltpu.VMEM((count, block, block), jnp.float32),
                 pltpu.VMEM((2, half, 8, block), jnp.float32),
                 pltpu.VMEM((half, 8, block), jnp.float32),
-                pltpu.VMEM((width, depth), jnp.bfloat16),
                 pltpu.SemaphoreType.DMA((chunks,)),
                 pltpu.SemaphoreType.DMA((chunks,)),
                 pltpu.SemaphoreType.DMA((chunks,)),
@@ -206,11 +210,12 @@
                 pltpu.SemaphoreType.DMA,
                 pltpu.SemaphoreType.DMA,
                 pltpu.SemaphoreType.DMA,
+                *[pltpu.VMEM((2, depth, width), jnp.bfloat16) for width in widths],
             ],
             compiler_params=pltpu.CompilerParams(
                 collective_id=0, has_side_effects=True, vmem_limit_bytes=50 * MIB
             ),
-        )(dosage, weights, blocks, flips.reshape(count, block))
+        )(dosage, weights, blocks.T, flips.reshape(count, block))
 
     in_specs = (P(("sec", "wide"), "grp"), P(None, "sec", None, None), P(None, "sec"), P("sec"))
     out_specs = P(("grp", "wide"), "sec")

time: 109 us -> 103 us (0.945)
  Pallas kernels: 105 us -> 100 us
  local copies, waits for them, and re-layouts: 3.74 us -> 2.36 us
    pallas_call x1, Pallas kernels: 105 us -> 100 us  [body(): pl.pallas_call(functools.partial(kernel, n, widths), out_shape=pltpu.VMEM...]
    unnamed x2 -> x1, local copies, waits for them, and re-layouts: 3.74 us -> 2.36 us
where the time goes in v2:
time: 103 us
  Pallas kernels  100 us (97%)
  local copies, waits for them, and re-layouts  2.36 us (2%)
    pallas_call x1, Pallas kernels, body(): pl.pallas_call(functools.partial(kernel, n, widths), out_shape=pltpu.VMEM...  100 us
    unnamed x1, local copies, waits for them, and re-layouts  2.36 us

profile of v2, /device:TPU:0, one launch (start us, length us, event | category | flops | bytes accessed | tf_op | source)
XLA Modules:
  0.0 102.6 jit_solution(7161692298390847956)
XLA Ops:
  0.0 100.2 %shard_map.46 = f32[1024,1280]{1,0:T(8,128)S(1)} custom-call(bf16[256,8192]{1,0:T(8,128)(2,1)} %dos.1, bf16[20,12,128,128]{3,2,1,0:T(8,128)(2,1)} %wts.1, s32[12,20]{1,0:T(8,128)} %bitcast.2, s32[16,128]{1,0:T(8,128)} %bitcast.3), custom_call_target="tpu_custom_call" | custom-call | tf_op jit(solution)/shard_map/pallas_call | solution.py:190
  100.2 2.4 %copy.6 = f32[1024,1280]{1,0:T(8,128)} copy(f32[1024,1280]{1,0:T(8,128)S(1)} %shard_map.46) | data formatting | bytes 10485760

commit v3 on v2

--- a/solution.py
+++ b/solution.py
@@ -46,6 +46,7 @@
     power = n & (n - 1) == 0
     order = list(range(1, n))
     peers = [partner_of(me, k) if power else lax.rem(me + k, n) for k in order]
+    near = n // 2 - 1
     mine = pl.ds(pl.multiple_of(me * rows, rows), rows)
 
     barrier = pltpu.get_barrier_semaphore()
@@ -68,12 +69,12 @@
     pl.semaphore_wait(barrier, n)
 
     for c in range(chunks):
-        for peer in peers:
+        for i, peer in enumerate(peers):
             pltpu.make_async_remote_copy(
                 src_ref=dos.at[:, pl.ds(pl.multiple_of(peer * samples + first_of[c], block), widths[c])],
                 dst_ref=x[c].at[sec, mine],
                 send_sem=send_sem.at[c],
-                recv_sem=recv_sem.at[c],
+                recv_sem=recv_sem.at[c, int(i >= near)],
                 device_id=(grp, peer, sec),
                 device_id_type=MESH,
             ).start()
@@ -151,19 +152,26 @@
 
         lax.fori_loop(0, columns // wide_n, column, 0)
 
+    def forward(c, owner):
+        there = x[c].at[sec, pl.ds(pl.multiple_of(owner * rows, rows), rows)]
+        pltpu.make_async_remote_copy(
+            src_ref=there, dst_ref=there, send_sem=fwd_send.at[c], recv_sem=fwd_recv.at[c],
+            device_id=(grp, me, other), device_id_type=MESH,
+        ).start()
+
     for c in range(chunks):
         own[c].wait()
-        from_peers = x[c].at[sec, pl.ds(0, (n - 1) * rows)]
-        pltpu.make_async_copy(from_peers, from_peers, recv_sem.at[c]).wait()
-        forward = pltpu.make_async_remote_copy(
-            src_ref=x[c].at[sec], dst_ref=x[c].at[sec], send_sem=fwd_send.at[c], recv_sem=fwd_recv.at[c],
-            device_id=(grp, me, other), device_id_type=MESH,
-        )
-        forward.start()
+        forward(c, me)
+        for g, group in enumerate((peers[:near], peers[near:])):
+            if group:
+                landed = x[c].at[sec, pl.ds(0, len(group) * rows)]
+                pltpu.make_async_copy(landed, landed, recv_sem.at[c, g]).wait()
+            for peer in group:
+                forward(c, peer)
         multiply(c, sec, True)
         pltpu.make_async_copy(x[c].at[sec], x[c].at[other], fwd_recv.at[c]).wait()
         multiply(c, other, False)
-        forward.wait_send()
+        pltpu.make_async_copy(x[c].at[sec], x[c].at[sec], fwd_send.at[c]).wait()
 
     for c in range(chunks):
         to_peers = x[c].at[sec, pl.ds(0, (n - 1) * rows)]
@@ -201,7 +209,7 @@
                 pltpu.VMEM((2, half, 8, block), jnp.float32),
                 pltpu.VMEM((half, 8, block), jnp.float32),
                 pltpu.SemaphoreType.DMA((chunks,)),
-                pltpu.SemaphoreType.DMA((chunks,)),
+                pltpu.SemaphoreType.DMA((chunks, 2)),
                 pltpu.SemaphoreType.DMA((chunks,)),
                 pltpu.SemaphoreType.DMA((chunks,)),
                 pltpu.SemaphoreType.DMA((chunks,)),

time: 103 us -> 103 us (level)
  no operation moved by 1% of the time
where the time goes in v3:
time: 103 us
  Pallas kernels  100 us (97%)
  local copies, waits for them, and re-layouts  2.36 us (2%)
    pallas_call x1, Pallas kernels, body(): pl.pallas_call(functools.partial(kernel, n, widths), out_shape=pltpu.VMEM...  100 us
    unnamed x1, local copies, waits for them, and re-layouts  2.36 us

profile of v3, /device:TPU:0, one launch (start us, length us, event | category | flops | bytes accessed | tf_op | source)
XLA Modules:
  0.0 102.6 jit_solution(10372258748339371564)
XLA Ops:
  0.0 100.2 %shard_map.46 = f32[1024,1280]{1,0:T(8,128)S(1)} custom-call(bf16[256,8192]{1,0:T(8,128)(2,1)} %dos.1, bf16[20,12,128,128]{3,2,1,0:T(8,128)(2,1)} %wts.1, s32[12,20]{1,0:T(8,128)} %bitcast.2, s32[16,128]{1,0:T(8,128)} %bitcast.3), custom_call_target="tpu_custom_call" | custom-call | tf_op jit(solution)/shard_map/pallas_call | solution.py:198
  100.2 2.4 %copy.6 = f32[1024,1280]{1,0:T(8,128)} copy(f32[1024,1280]{1,0:T(8,128)S(1)} %shard_map.46) | data formatting | bytes 10485760
